TPU v7x, 128 devices: a whole 4x4x4 slice. The times are simulated.
128 devices in a mesh: chan: 16 (over y, x), tm: 8 (over z, core).
Axes of the slice: x: 4, y: 4, z: 4, core: 2. Of those that a mesh axis runs over, the one named last changes fastest.
Arguments:
- samples: bfloat16 [256, 192, 4096], P('chan', 'tm'), may hold values from -6 to 6
- taps: float32 [16, 4096], replicated, may hold values from -1.5 to 1.5
- block_tile: int32 [120], replicated, may hold values from 0 to 15, as said below
- tile_slots: int32 [16], replicated, may hold values from 0 to 15, as said below
- kern_u: bfloat16 [16, 30720], replicated, may hold values from -1.1953125 to 1.1953125
- kern_v: bfloat16 [16, 30720], replicated, may hold values from -1.1953125 to 1.1953125
Outputs:
- uv_grid: float32 [16, 2048, 2, 256], P('tm', 'chan')
Inputs may be any that keep to these rules, and one draw needn't show every extreme that they name: `block_tile`: A tile's owner is (its position in tile_slots) // 2. The blocks that fall in the tiles of one owner are at most 30; in every draw one owner has exactly 30. `tile_slots`: each tile number stands once.
All inputs are finite; a program needn't handle non-finite values.
Results may differ from a plain program's by a relative error of at most 0.0077.
Values may be sent and summed in bfloat16 or wider, within the bound.
No kernel may reach another device: no remote copies, remote signals or barrier semaphores. Data moves between devices by JAX's collectives and lax.ppermute only.
A program may use at most 192 MiB of HBM per device.

v0:
```python
import math
import jax
import jax.numpy as jnp
import numpy as np
from jax import lax
from jax.sharding import PartitionSpec as P

SBLK = 16
GRID = 16


def passed_along(value, axis, steps):
    count = lax.axis_size(axis)
    leading, last = (max(0, -steps), min(count, count - steps))
    return lax.ppermute(value, axis, [(source, source + steps) for source in range(leading, last)])


def block_pairs(block_total):
    left_list = []
    right_list = []
    for p in range(block_total):
        for q in range(p + 1, block_total):
            left_list.append(p)
            right_list.append(q)
    return (np.array(left_list, dtype=np.int32), np.array(right_list, dtype=np.int32))


def make_kernel(u_part, v_part, block_total):
    u_cols = u_part.astype(jnp.float32).reshape(GRID, block_total, SBLK * SBLK).transpose(1, 2, 0)
    v_cols = v_part.astype(jnp.float32).reshape(GRID, block_total, SBLK * SBLK).transpose(1, 2, 0)
    product = u_cols[:, :, :, None] * v_cols[:, :, None, :]
    return product.reshape(block_total, SBLK * SBLK, GRID * GRID).astype(jnp.bfloat16)


def body(samples, taps, block_tile, tile_slots, kern_u, kern_v):
    station_count, frame_count, length = samples.shape
    channel_count = length // 2
    chan_size = lax.axis_size("chan")
    tm_size = lax.axis_size("tm")
    group_count = chan_size * tm_size
    group_width = channel_count // group_count
    tap_count = taps.shape[0]
    history = passed_along(samples[:, frame_count - (tap_count - 1) :], "tm", 1)
    padded = jnp.concatenate([history, samples], axis=1)
    filtered = jnp.zeros((station_count, frame_count, length), jnp.float32)
    for tap_index in range(tap_count):
        offset = tap_count - 1 - tap_index
        filtered = filtered + taps[tap_index] * padded[:, offset : offset + frame_count].astype(
            jnp.float32
        )
    rows_in = filtered.astype(jnp.bfloat16).reshape(station_count * frame_count, length)
    dft_scale = 1.0 / math.sqrt(length)
    block_cols = min(channel_count, 256)
    groups_per_block = block_cols // group_width
    positions = jnp.arange(length, dtype=jnp.int32)[:, None, None]
    pieces = []
    for column_block in range(channel_count // block_cols):
        channels = column_block * block_cols + jnp.arange(block_cols, dtype=jnp.int32).reshape(
            1, groups_per_block, group_width
        )
        phase_int = positions * channels % length
        phase_angle = phase_int.astype(jnp.float32) * (2.0 * math.pi / length)
        cosine = jnp.cos(phase_angle).astype(jnp.bfloat16)
        sine_neg = (-jnp.sin(phase_angle)).astype(jnp.bfloat16)
        dft_table = jnp.stack([cosine, sine_neg], axis=2).reshape(length, 2 * block_cols)
        spectrum = (
            lax.dot_general(
                dft_table, rows_in, (((0,), (1,)), ((), ())), preferred_element_type=jnp.float32
            )
            * dft_scale
        )
        pieces.append(
            spectrum.astype(jnp.bfloat16).reshape(
                groups_per_block, 2, group_width, station_count, frame_count
            )
        )
    spectra = jnp.concatenate(pieces, axis=0)
    stations = station_count * chan_size
    frames = frame_count * tm_size
    arranged = spectra.reshape(chan_size, tm_size, 2, group_width, station_count, frame_count)
    turned = lax.all_to_all(
        lax.all_to_all(arranged, "chan", split_axis=0, concat_axis=4, tiled=True),
        "tm",
        split_axis=1,
        concat_axis=5,
        tiled=True,
    )
    turned = turned.reshape(2, group_width, stations, frames)
    block_rows = stations // SBLK
    block_total = block_rows * (block_rows - 1) // 2
    vis_scale = 1.0 / math.sqrt(frames)
    swapped = jnp.stack([turned[1], -turned[0]], axis=0)
    real_part = (
        jnp.einsum("cgib,cgjb->gij", turned, turned, preferred_element_type=jnp.float32) * vis_scale
    )
    imag_part = (
        jnp.einsum("cgib,cgjb->gij", swapped, turned, preferred_element_type=jnp.float32)
        * vis_scale
    )
    left_idx, right_idx = block_pairs(block_rows)
    visibility = jnp.stack([real_part, imag_part], axis=1).reshape(
        group_width, 2, block_rows, SBLK, block_rows, SBLK
    )
    visibility = visibility[:, :, left_idx, :, right_idx, :]
    blocks = visibility.reshape(block_total, group_width, 2, SBLK * SBLK).astype(jnp.bfloat16)
    tile_count = tile_slots.shape[0]
    slot_ids = jnp.arange(tile_count, dtype=jnp.int32)
    tile_match = block_tile[:, None] == tile_slots[None, :]
    slot_of_block = jnp.sum(jnp.where(tile_match, slot_ids[None, :], 0), axis=1)
    kernel = make_kernel(kern_u, kern_v, block_total)
    per_block = jnp.einsum("mgce,mel->mgcl", blocks, kernel, preferred_element_type=jnp.float32)
    slot_hits = (slot_of_block[:, None] == slot_ids[None, :]).astype(jnp.float32)
    partial_value = jnp.einsum(
        "mgcl,ms->sgcl", per_block, slot_hits, precision=lax.Precision.HIGHEST
    )
    uv_grid = lax.all_to_all(partial_value, "tm", split_axis=0, concat_axis=1, tiled=True)
    return uv_grid


def solution(mesh):
    placed = (P("chan", "tm", None), P(), P(), P(), P(), P())
    return jax.shard_map(
        body, mesh=mesh, in_specs=placed, out_specs=P("tm", "chan", None, None), check_vma=False
    )
```

profile of v0, /device:TPU:1, one launch (start us, length us, event | category | flops | bytes accessed | tf_op | source)
XLA Modules:
  0.0 647.3 jit_solution(4451937538021533933)
XLA Ops:
  9.7 18.1 %cosine_convert_fusion.7 = (bf16[4096,16,1,16]{0,3,2,1:T(8,128)(2,1)S(1)}, bf16[4096,16,1,16]{0,3,2,1:T(8,128)(2,1)S(1)}) fusion(s32[16,16]{1,0:T(8,128)S(1)} %multiply_add_fusion), kind=kLoop, calls=%fused_computation.119 | loop fusion | flops 17825792 | bytes 4195328 | tf_op jit(solution)/shard_map/convert_element_type | solution.py:63
  27.7 18.1 %cosine_convert_fusion.6 = (bf16[4096,16,1,16]{0,3,2,1:T(8,128)(2,1)S(1)}, bf16[4096,16,1,16]{0,3,2,1:T(8,128)(2,1)S(1)}) fusion(s32[16,16]{1,0:T(8,128)S(1)} %fusion.84), kind=kLoop, calls=%fused_computation.115 | loop fusion | flops 17825792 | bytes 4195328 | tf_op jit(solution)/shard_map/convert_element_type | solution.py:63
  45.8 18.1 %cosine_convert_fusion.5 = (bf16[4096,16,1,16]{0,3,2,1:T(8,128)(2,1)S(1)}, bf16[4096,16,1,16]{0,3,2,1:T(8,128)(2,1)S(1)}) fusion(s32[16,16]{1,0:T(8,128)S(1)} %fusion.83), kind=kLoop, calls=%fused_computation.111 | loop fusion | flops 17825792 | bytes 4195328 | tf_op jit(solution)/shard_map/convert_element_type | solution.py:63
  63.9 18.1 %cosine_convert_fusion.4 = (bf16[4096,16,1,16]{0,3,2,1:T(8,128)(2,1)S(1)}, bf16[4096,16,1,16]{0,3,2,1:T(8,128)(2,1)S(1)}) fusion(s32[16,16]{1,0:T(8,128)S(1)} %fusion.82), kind=kLoop, calls=%fused_computation.107 | loop fusion | flops 17825792 | bytes 4195328 | tf_op jit(solution)/shard_map/convert_element_type | solution.py:63
  82.0 18.1 %cosine_convert_fusion.3 = (bf16[4096,16,1,16]{0,3,2,1:T(8,128)(2,1)S(1)}, bf16[4096,16,1,16]{0,3,2,1:T(8,128)(2,1)S(1)}) fusion(s32[16,16]{1,0:T(8,128)S(1)} %fusion.81), kind=kLoop, calls=%fused_computation.103 | loop fusion | flops 17825792 | bytes 4195328 | tf_op jit(solution)/shard_map/convert_element_type | solution.py:63
  100.0 18.1 %cosine_convert_fusion.2 = (bf16[4096,16,1,16]{0,3,2,1:T(8,128)(2,1)S(1)}, bf16[4096,16,1,16]{0,3,2,1:T(8,128)(2,1)S(1)}) fusion(s32[16,16]{1,0:T(8,128)S(1)} %fusion.80), kind=kLoop, calls=%fused_computation.99 | loop fusion | flops 17825792 | bytes 4195328 | tf_op jit(solution)/shard_map/convert_element_type | solution.py:63
  118.1 18.1 %cosine_convert_fusion.1 = (bf16[4096,16,1,16]{0,3,2,1:T(8,128)(2,1)S(1)}, bf16[4096,16,1,16]{0,3,2,1:T(8,128)(2,1)S(1)}) fusion(s32[16,16]{1,0:T(8,128)S(1)} %fusion.79), kind=kLoop, calls=%fused_computation.95 | loop fusion | flops 17825792 | bytes 4195328 | tf_op jit(solution)/shard_map/convert_element_type | solution.py:63
  136.2 19.0 %cosine_convert_fusion = (bf16[4096,16,1,16]{0,3,2,1:T(8,128)(2,1)S(1)}, bf16[4096,16,1,16]{0,3,2,1:T(8,128)(2,1)}) fusion(s32[16,16]{1,0:T(8,128)S(1)} %fusion.78), kind=kLoop, calls=%fused_computation.91 | loop fusion | flops 17825792 | bytes 4195328 | tf_op jit(solution)/shard_map/convert_element_type | solution.py:63
  178.3 23.2 %add_convert_fusion = bf16[16,24,4096]{2,1,0:T(8,128)(2,1)} fusion(bf16[16,24,4096]{2,1,0:T(8,128)(2,1)S(1)} %copy-done, bf16[16,15,4096]{2,1,0:T(8,128)(2,1)} %copy.81, f32[4096]{0:T(1024)S(1)} %bitcast.136, f32[4096]{0:T(1024)S(1)} %bitcast.137, f32[4096]{0:T(1024)S(1)} %bitcast.123, f32[4096]{0:T(1024)S(1)} %bitcast.124, f32[4096]{0:T(1024)S(1)} %bitcast.125, ...), kind=kLoop, calls=%fused_computation.52 | loop fusion | flops 146276352 | bytes 8519680 | tf_op jit(solution)/shard_map/convert_element_type | solution.py:51
  201.5 5.5 fusion.70
  220.1 5.5 fusion.72
  238.5 5.5 fusion.74
  247.8 5.5 fusion.75
  257.2 5.5 fusion.76
  266.4 5.5 fusion.77
  288.1 22.6 %reshape.779 = bf16[16,2,49152]{2,1,0:T(2,128)(2,1)S(1)} reshape(bf16[16,8,2,16,16,24]{5,4,3,2,1,0:T(8,128)(2,1)} %bitcast.96) | data formatting | bytes 6291456
  310.7 47.5 %all_to_all.51 = bf16[16,2,49152]{2,1,0:T(2,128)(2,1)} all-to-all(bf16[16,2,49152]{2,1,0:T(2,128)(2,1)S(1)} %reshape.779), channel_id=1, replica_groups=mesh['chan'=16,'tm'=8] {'chan'}, dimensions={0} | all-to-all | bytes 6291456 | tf_op jit(solution)/shard_map/all_to_all | solution.py:82
  358.2 25.0 %reshape.780 = bf16[16,8,2,16,16,24]{5,4,3,2,1,0:T(8,128)(2,1)} reshape(bf16[16,2,49152]{2,1,0:T(2,128)(2,1)} %all_to_all.51) | data formatting | bytes 6291456
  383.2 32.4 %copy.82 = bf16[1,8,2,16,16,16,24]{5,4,6,3,2,1,0:T(8,128)(2,1)} copy(bf16[1,8,2,16,16,16,24]{6,5,3,2,1,4,0:T(8,128)(2,1)} %bitcast.92) | data formatting | bytes 6291456 | tf_op jit(solution)/shard_map/all_to_all | solution.py:82
  415.6 30.1 %all_to_all.40 = bf16[1,8,2,16,256,24]{4,5,3,2,1,0:T(8,128)(2,1)} reshape(bf16[1,8,2,16,16,16,24]{5,4,6,3,2,1,0:T(8,128)(2,1)} %copy.82) | data formatting | bytes 6291456 | tf_op jit(solution)/shard_map/all_to_all | solution.py:82
  453.6 8.7 %multiply_convert_fusion = bf16[120,256,16,16]{1,3,2,0:T(8,128)(2,1)} fusion(f32[120,256,16]{1,2,0:T(8,128)S(1)} %get-tuple-element.39, f32[120,256,16]{1,2,0:T(8,128)S(1)} %get-tuple-element.40), kind=kLoop, calls=%fused_computation.2 | loop fusion | flops 15728640 | bytes 19660800 | tf_op jit(solution)/shard_map/convert_element_type | solution.py:32
  462.2 25.4 %all-to-all-done.1 = bf16[1,8,2,16,256,24]{4,5,3,2,0,1:T(8,128)(2,1)S(1)} async-done(((bf16[1,8,2,16,256,24]{4,5,3,2,0,1:T(8,128)(2,1)}), bf16[1,8,2,16,256,24]{4,5,3,2,0,1:T(8,128)(2,1)S(1)}, u32[]{:S(2)}, u32[]{:S(2)}) %all-to-all-start.1) | async-done | bytes 3145760 | tf_op jit(solution)/shard_map/all_to_all | solution.py:81
  492.8 17.4 %stack.63 = bf16[16,1,16,16,16,16]{5,4,3,2,0,1:T(8,128)(2,1)} reshape(bf16[16,256,256]{2,1,0:T(8,128)(2,1)} %bitcast_multiply_fusion) | data formatting | bytes 4194304 | tf_op jit(solution)/shard_map/stack | solution.py:101
  510.2 16.6 %copy.88 = bf16[16,1,16,16,16,16]{5,3,4,2,1,0:T(8,128)(2,1)} copy(bf16[16,1,16,16,16,16]{5,4,3,2,0,1:T(8,128)(2,1)} %stack.63) | data formatting | bytes 4194304 | tf_op jit(solution)/shard_map/stack | solution.py:101
  526.9 14.3 %stack.61 = bf16[16,1,16,16,16,16]{5,4,3,2,0,1:T(8,128)(2,1)} reshape(bf16[16,256,256]{2,1,0:T(8,128)(2,1)S(1)} %bitcast_multiply_fusion.1) | data formatting | bytes 4194304 | tf_op jit(solution)/shard_map/stack | solution.py:101
  541.2 16.6 %copy.87 = bf16[16,1,16,16,16,16]{5,3,4,2,1,0:T(8,128)(2,1)} copy(bf16[16,1,16,16,16,16]{5,4,3,2,0,1:T(8,128)(2,1)} %stack.61) | data formatting | bytes 4194304 | tf_op jit(solution)/shard_map/stack | solution.py:101
  557.8 22.7 %pad_maximum_fusion = bf16[16,2,16,16,16,16]{5,3,4,2,1,0:T(8,128)(2,1)} fusion(bf16[16,1,16,16,16,16]{5,3,4,2,1,0:T(8,128)(2,1)} %copy.88, bf16[16,1,16,16,16,16]{5,3,4,2,1,0:T(8,128)(2,1)} %copy.87), kind=kLoop, calls=%fused_computation.1 | loop fusion | flops 2097152 | bytes 8388608 | tf_op jit(solution)/shard_map/stack | solution.py:101
  580.5 12.2 %gather_fusion = bf16[120,16,2,16,16]{4,3,2,1,0:T(8,128)(2,1)} fusion(bf16[16,2,16,16,16,16]{5,3,4,2,1,0:T(8,128)(2,1)} %pad_maximum_fusion, s32[120]{0:T(128)S(1)} %copy-done.8), kind=kCustom, calls=%fused_computation | custom fusion | bytes 3933120 | tf_op jit(solution)/shard_map/gather | solution.py:104
  592.7 18.3 %copy.89 = bf16[120,16,2,16,16]{0,4,3,2,1:T(8,128)(2,1)S(1)} copy(bf16[120,16,2,16,16]{4,3,2,1,0:T(8,128)(2,1)} %gather_fusion) | data formatting | bytes 3932160 | tf_op jit(solution)/shard_map/gather | solution.py:104
  614.3 12.6 %fusion.91 = f32[120,16,2,256]{3,1,2,0:T(8,128)} fusion(bf16[120,16,2,256]{3,1,2,0:T(8,128)(2,1)} %copy.92, bf16[120,256,256,1]{1,2,3,0:T(8,128)(2,1)} %bitcast.93), kind=kOutput, calls=%fused_computation.193 | convolution fusion | flops 503316480 | bytes 21626880 | tf_op jit(solution)/shard_map/mgce,mel->mgcl/dot_general | solution.py:111
  626.9 5.8 fusion.48
  633.2 12.6 %all_to_all.52 = f32[16,16,2,256]{3,2,1,0:T(2,128)S(1)} all-to-all(f32[16,16,2,256]{3,2,1,0:T(2,128)S(1)} %copy.95), channel_id=1, replica_groups=mesh['chan'=16,'tm'=8] {'tm'}, dimensions={0} | all-to-all | bytes 1048576 | tf_op jit(solution)/shard_map/all_to_all | solution.py:116
  (80 shorter events, 103.6 us)
Async XLA Ops:
  4.6 169.6 %collective-permute-start = (bf16[16,15,4096]{2,0,1:T(8,128)(2,1)}, bf16[16,15,4096]{2,0,1:T(8,128)(2,1)}, u32[]{:S(2)}, u32[]{:S(2)}) collective-permute-start(bf16[16,15,4096]{2,0,1:T(8,128)(2,1)} %copy.103), channel_id=1, source_target_pairs={{0,1},{1,2},{2,3},{3,4},{4,5},{5,6},{6,7},{8,9},{9,10},{10,11},{11... | collective-permute-start | bytes 5898248 | tf_op jit(solution)/shard_map/ppermute | solution.py:15
  169.3 2.3 copy-start.7
  171.6 2.4 copy-start.10
  174.0 4.4 copy-start
  209.8 2.9 copy-start.9
  275.6 2.2 copy-start.1
  275.6 3.9 copy-start.2
  277.8 3.4 copy-start.3
  279.5 3.5 copy-start.4
  281.2 3.5 copy-start.5
  283.0 3.4 copy-start.6
  445.7 42.0 %all-to-all-start.1 = ((bf16[1,8,2,16,256,24]{4,5,3,2,0,1:T(8,128)(2,1)}), bf16[1,8,2,16,256,24]{4,5,3,2,0,1:T(8,128)(2,1)S(1)}, u32[]{:S(2)}, u32[]{:S(2)}) async-start(bf16[1,8,2,16,256,24]{4,5,3,2,0,1:T(8,128)(2,1)} %bitcast.97), calls=%async_computation.1 | async-start | bytes 6291456 | tf_op jit(solution)/shard_map/all_to_all | solution.py:81
  450.1 2.7 copy-start.11
  450.1 2.7 copy-start.12
  557.8 22.7 %copy-start.8 = (s32[120]{0:T(128)S(1)}, s32[120]{0:T(128)}, u32[]{:S(2)}) copy-start(s32[120]{0:T(128)} %constant.106) | copy-start | bytes 1444
where the time goes:
time: 658 us; the launch traced here: 647 us
  local copies, waits for them, and re-layouts  264 us (40%)
  other arithmetic  222 us (34%)
  matrix products  65.5 us (10%)
  blocking collectives  60.1 us (9%)
  waiting for transfers between devices  25.4 us (4%)
  starting transfers between devices  9.37 us (1%)
    convert_element_type x8, other arithmetic, body(): cosine = jnp.cos(phase_angle).astype(jnp.bfloat16)  145 us
    another operation x4, local copies, waits for them, and re-layouts, body(): jnp.stack([real_part, imag_part], axis=1)  65 us
    unnamed x36, local copies, waits for them, and re-layouts  63.9 us
    all_to_all x2, local copies, waits for them, and re-layouts, body(): lax.all_to_all(arranged, 'chan', split_axis=0, concat_axis=4, tiled=True)  62.5 us
    all_to_all x1, blocking collectives, body(): lax.all_to_all(arranged, 'chan', split_axis=0, concat_axis=4, tiled=True)  47.5 us
    dot_general x8, matrix products, body(): lax.dot_general(dft_table, rows_in, (((0,), (1,)), ((), ())), preferred_e...  42.9 us
    gather x2, local copies, waits for them, and re-layouts, body(): visibility = visibility[:, :, left_idx, :, right_idx, :]  30.6 us
    reshape x8, local copies, waits for them, and re-layouts, body(): spectrum.astype(jnp.bfloat16)  28.2 us
  transfers between devices with their start and end apart: 2, of which 1 were waited for; matrix products, arithmetic and copies ran while one was open for 27% of the time, Pallas kernels for 0%

commit v1 on v0

--- a/solution.py
+++ b/solution.py
@@ -78,12 +78,20 @@
     stations = station_count * chan_size
     frames = frame_count * tm_size
     arranged = spectra.reshape(chan_size, tm_size, 2, group_width, station_count, frame_count)
-    turned = lax.all_to_all(
-        lax.all_to_all(arranged, "chan", split_axis=0, concat_axis=4, tiled=True),
-        "tm",
-        split_axis=1,
-        concat_axis=5,
-        tiled=True,
+    turned = jnp.concatenate(
+        lax.all_to_all(
+            jnp.stack(
+                jnp.split(
+                    lax.all_to_all(arranged, "chan", split_axis=0, concat_axis=4, tiled=True),
+                    lax.axis_size("tm"),
+                    axis=1,
+                )
+            ),
+            "tm",
+            0,
+            0,
+        ),
+        axis=5,
     )
     turned = turned.reshape(2, group_width, stations, frames)
     block_rows = stations // SBLK

time: 658 us -> 663 us (level)
    unnamed x36 -> x43, local copies, waits for them, and re-layouts: 63.9 us -> 69.3 us
where the time goes in v1:
time: 663 us; the launch traced here: 652 us
  local copies, waits for them, and re-layouts  269 us (41%)
  other arithmetic  222 us (33%)
  matrix products  65.5 us (10%)
  blocking collectives  60.1 us (9%)
  waiting for transfers between devices  25.4 us (4%)
  starting transfers between devices  9.37 us (1%)
    convert_element_type x8, other arithmetic, body(): cosine = jnp.cos(phase_angle).astype(jnp.bfloat16)  145 us
    unnamed x43, local copies, waits for them, and re-layouts  69.3 us
    another operation x4, local copies, waits for them, and re-layouts, body(): jnp.stack([real_part, imag_part], axis=1)  65 us
    all_to_all x2, local copies, waits for them, and re-layouts, body(): lax.all_to_all(arranged, 'chan', split_axis=0, concat_axis=4, tiled=True)  60.9 us
    all_to_all x1, blocking collectives, body(): lax.all_to_all(arranged, 'chan', split_axis=0, concat_axis=4, tiled=True)  47.5 us
    dot_general x8, matrix products, body(): lax.dot_general(dft_table, rows_in, (((0,), (1,)), ((), ())), preferred_e...  42.9 us
    gather x2, local copies, waits for them, and re-layouts, body(): visibility = visibility[:, :, left_idx, :, right_idx, :]  30.6 us
    reshape x8, local copies, waits for them, and re-layouts, body(): spectrum.astype(jnp.bfloat16)  28.2 us
  transfers between devices with their start and end apart: 2, of which 1 were waited for; matrix products, arithmetic and copies ran while one was open for 27% of the time, Pallas kernels for 0%

profile of v1, /device:TPU:1, one launch (start us, length us, event | category | flops | bytes accessed | tf_op | source)
XLA Modules:
  0.0 651.9 jit_solution(15957559578955189802)
XLA Ops:
  9.7 18.1 %cosine_convert_fusion.7 = (bf16[4096,16,1,16]{0,3,2,1:T(8,128)(2,1)S(1)}, bf16[4096,16,1,16]{0,3,2,1:T(8,128)(2,1)S(1)}) fusion(s32[16,16]{1,0:T(8,128)S(1)} %multiply_add_fusion), kind=kLoop, calls=%fused_computation.119 | loop fusion | flops 17825792 | bytes 4195328 | tf_op jit(solution)/shard_map/convert_element_type | solution.py:63
  27.7 18.1 %cosine_convert_fusion.6 = (bf16[4096,16,1,16]{0,3,2,1:T(8,128)(2,1)S(1)}, bf16[4096,16,1,16]{0,3,2,1:T(8,128)(2,1)S(1)}) fusion(s32[16,16]{1,0:T(8,128)S(1)} %fusion.92), kind=kLoop, calls=%fused_computation.115 | loop fusion | flops 17825792 | bytes 4195328 | tf_op jit(solution)/shard_map/convert_element_type | solution.py:63
  45.8 18.1 %cosine_convert_fusion.5 = (bf16[4096,16,1,16]{0,3,2,1:T(8,128)(2,1)S(1)}, bf16[4096,16,1,16]{0,3,2,1:T(8,128)(2,1)S(1)}) fusion(s32[16,16]{1,0:T(8,128)S(1)} %fusion.91), kind=kLoop, calls=%fused_computation.111 | loop fusion | flops 17825792 | bytes 4195328 | tf_op jit(solution)/shard_map/convert_element_type | solution.py:63
  63.9 18.1 %cosine_convert_fusion.4 = (bf16[4096,16,1,16]{0,3,2,1:T(8,128)(2,1)S(1)}, bf16[4096,16,1,16]{0,3,2,1:T(8,128)(2,1)S(1)}) fusion(s32[16,16]{1,0:T(8,128)S(1)} %fusion.90), kind=kLoop, calls=%fused_computation.107 | loop fusion | flops 17825792 | bytes 4195328 | tf_op jit(solution)/shard_map/convert_element_type | solution.py:63
  82.0 18.1 %cosine_convert_fusion.3 = (bf16[4096,16,1,16]{0,3,2,1:T(8,128)(2,1)S(1)}, bf16[4096,16,1,16]{0,3,2,1:T(8,128)(2,1)S(1)}) fusion(s32[16,16]{1,0:T(8,128)S(1)} %fusion.89), kind=kLoop, calls=%fused_computation.103 | loop fusion | flops 17825792 | bytes 4195328 | tf_op jit(solution)/shard_map/convert_element_type | solution.py:63
  100.0 18.1 %cosine_convert_fusion.2 = (bf16[4096,16,1,16]{0,3,2,1:T(8,128)(2,1)S(1)}, bf16[4096,16,1,16]{0,3,2,1:T(8,128)(2,1)S(1)}) fusion(s32[16,16]{1,0:T(8,128)S(1)} %fusion.88), kind=kLoop, calls=%fused_computation.99 | loop fusion | flops 17825792 | bytes 4195328 | tf_op jit(solution)/shard_map/convert_element_type | solution.py:63
  118.1 18.1 %cosine_convert_fusion.1 = (bf16[4096,16,1,16]{0,3,2,1:T(8,128)(2,1)S(1)}, bf16[4096,16,1,16]{0,3,2,1:T(8,128)(2,1)S(1)}) fusion(s32[16,16]{1,0:T(8,128)S(1)} %fusion.87), kind=kLoop, calls=%fused_computation.95 | loop fusion | flops 17825792 | bytes 4195328 | tf_op jit(solution)/shard_map/convert_element_type | solution.py:63
  136.2 19.0 %cosine_convert_fusion = (bf16[4096,16,1,16]{0,3,2,1:T(8,128)(2,1)S(1)}, bf16[4096,16,1,16]{0,3,2,1:T(8,128)(2,1)}) fusion(s32[16,16]{1,0:T(8,128)S(1)} %fusion.86), kind=kLoop, calls=%fused_computation.91 | loop fusion | flops 17825792 | bytes 4195328 | tf_op jit(solution)/shard_map/convert_element_type | solution.py:63
  178.3 23.2 %add_convert_fusion = bf16[16,24,4096]{2,1,0:T(8,128)(2,1)} fusion(bf16[16,24,4096]{2,1,0:T(8,128)(2,1)S(1)} %copy-done, bf16[16,15,4096]{2,1,0:T(8,128)(2,1)} %copy.86, f32[4096]{0:T(1024)S(1)} %bitcast.164, f32[4096]{0:T(1024)S(1)} %bitcast.165, f32[4096]{0:T(1024)S(1)} %bitcast.151, f32[4096]{0:T(1024)S(1)} %bitcast.152, f32[4096]{0:T(1024)S(1)} %bitcast.153, ...), kind=kLoop, calls=%fused_computation.52 | loop fusion | flops 146276352 | bytes 8519680 | tf_op jit(solution)/shard_map/convert_element_type | solution.py:51
  201.5 5.5 fusion.70
  220.1 5.5 fusion.72
  238.5 5.5 fusion.74
  247.8 5.5 fusion.75
  257.2 5.5 fusion.76
  266.4 5.5 fusion.77
  288.1 22.6 %reshape.778 = bf16[16,2,49152]{2,1,0:T(2,128)(2,1)S(1)} reshape(bf16[16,8,2,16,16,24]{5,4,3,2,1,0:T(8,128)(2,1)} %bitcast.125) | data formatting | bytes 6291456
  310.7 47.5 %all_to_all.41 = bf16[16,2,49152]{2,1,0:T(2,128)(2,1)} all-to-all(bf16[16,2,49152]{2,1,0:T(2,128)(2,1)S(1)} %reshape.778), channel_id=1, replica_groups=mesh['chan'=16,'tm'=8] {'chan'}, dimensions={0} | all-to-all | bytes 6291456 | tf_op jit(solution)/shard_map/all_to_all | solution.py:85
  358.2 25.0 %reshape.779 = bf16[16,8,2,16,16,24]{5,4,3,2,1,0:T(8,128)(2,1)} reshape(bf16[16,2,49152]{2,1,0:T(2,128)(2,1)} %all_to_all.41) | data formatting | bytes 6291456
  383.2 32.4 %copy.87 = bf16[1,8,2,16,16,16,24]{5,4,6,3,2,1,0:T(8,128)(2,1)} copy(bf16[1,8,2,16,16,16,24]{6,5,3,2,1,4,0:T(8,128)(2,1)} %bitcast.121) | data formatting | bytes 6291456 | tf_op jit(solution)/shard_map/all_to_all | solution.py:85
  415.6 28.5 %all_to_all.32 = bf16[1,8,2,16,256,24]{4,5,3,2,1,0:T(8,128)(2,1)S(1)} reshape(bf16[1,8,2,16,16,16,24]{5,4,6,3,2,1,0:T(8,128)(2,1)} %copy.87) | data formatting | bytes 6291456 | tf_op jit(solution)/shard_map/all_to_all | solution.py:85
  458.2 8.7 %multiply_convert_fusion = bf16[120,256,16,16]{1,3,2,0:T(8,128)(2,1)} fusion(f32[120,256,16]{1,2,0:T(8,128)S(1)} %get-tuple-element.39, f32[120,256,16]{1,2,0:T(8,128)S(1)} %get-tuple-element.40), kind=kLoop, calls=%fused_computation.2 | loop fusion | flops 15728640 | bytes 19660800 | tf_op jit(solution)/shard_map/convert_element_type | solution.py:32
  466.9 25.4 %all-to-all-done.1 = bf16[8,1,1,2,16,256,24]{5,6,4,3,2,1,0:T(8,128)(2,1)S(1)} async-done(((bf16[8,1,1,2,16,256,24]{5,6,4,3,2,1,0:T(8,128)(2,1)}), bf16[8,1,1,2,16,256,24]{5,6,4,3,2,1,0:T(8,128)(2,1)S(1)}, u32[]{:S(2)}, u32[]{:S(2)}) %all-to-all-start.1) | async-done | bytes 3145760 | tf_op jit(solution)/shard_map/all_to_all | solution.py:82
  497.5 17.4 %stack.99 = bf16[16,1,16,16,16,16]{5,4,3,2,0,1:T(8,128)(2,1)} reshape(bf16[16,256,256]{2,1,0:T(8,128)(2,1)} %bitcast_multiply_fusion) | data formatting | bytes 4194304 | tf_op jit(solution)/shard_map/stack | solution.py:109
  514.9 16.6 %copy.92 = bf16[16,1,16,16,16,16]{5,3,4,2,1,0:T(8,128)(2,1)} copy(bf16[16,1,16,16,16,16]{5,4,3,2,0,1:T(8,128)(2,1)} %stack.99) | data formatting | bytes 4194304 | tf_op jit(solution)/shard_map/stack | solution.py:109
  531.6 14.3 %stack.97 = bf16[16,1,16,16,16,16]{5,4,3,2,0,1:T(8,128)(2,1)} reshape(bf16[16,256,256]{2,1,0:T(8,128)(2,1)S(1)} %bitcast_multiply_fusion.1) | data formatting | bytes 4194304 | tf_op jit(solution)/shard_map/stack | solution.py:109
  545.9 16.6 %copy.91 = bf16[16,1,16,16,16,16]{5,3,4,2,1,0:T(8,128)(2,1)} copy(bf16[16,1,16,16,16,16]{5,4,3,2,0,1:T(8,128)(2,1)} %stack.97) | data formatting | bytes 4194304 | tf_op jit(solution)/shard_map/stack | solution.py:109
  562.5 22.7 %pad_maximum_fusion = bf16[16,2,16,16,16,16]{5,3,4,2,1,0:T(8,128)(2,1)} fusion(bf16[16,1,16,16,16,16]{5,3,4,2,1,0:T(8,128)(2,1)} %copy.92, bf16[16,1,16,16,16,16]{5,3,4,2,1,0:T(8,128)(2,1)} %copy.91), kind=kLoop, calls=%fused_computation.1 | loop fusion | flops 2097152 | bytes 8388608 | tf_op jit(solution)/shard_map/stack | solution.py:109
  585.2 12.2 %gather_fusion = bf16[120,16,2,16,16]{4,3,2,1,0:T(8,128)(2,1)} fusion(bf16[16,2,16,16,16,16]{5,3,4,2,1,0:T(8,128)(2,1)} %pad_maximum_fusion, s32[120]{0:T(128)S(1)} %copy-done.8), kind=kCustom, calls=%fused_computation | custom fusion | bytes 3933120 | tf_op jit(solution)/shard_map/gather | solution.py:112
  597.4 18.3 %copy.93 = bf16[120,16,2,16,16]{0,4,3,2,1:T(8,128)(2,1)S(1)} copy(bf16[120,16,2,16,16]{4,3,2,1,0:T(8,128)(2,1)} %gather_fusion) | data formatting | bytes 3932160 | tf_op jit(solution)/shard_map/gather | solution.py:112
  619.0 12.6 %fusion.99 = f32[120,16,2,256]{3,1,2,0:T(8,128)} fusion(bf16[120,16,2,256]{3,1,2,0:T(8,128)(2,1)} %copy.96, bf16[120,256,256,1]{1,2,3,0:T(8,128)(2,1)} %bitcast.122), kind=kOutput, calls=%fused_computation.209 | convolution fusion | flops 503316480 | bytes 21626880 | tf_op jit(solution)/shard_map/mgce,mel->mgcl/dot_general | solution.py:119
  631.6 5.8 fusion.48
  637.8 12.6 %all_to_all.42 = f32[16,16,2,256]{3,2,1,0:T(2,128)S(1)} all-to-all(f32[16,16,2,256]{3,2,1,0:T(2,128)S(1)} %copy.99), channel_id=1, replica_groups=mesh['chan'=16,'tm'=8] {'tm'}, dimensions={0} | all-to-all | bytes 1048576 | tf_op jit(solution)/shard_map/all_to_all | solution.py:124
  (88 shorter events, 109.9 us)
Async XLA Ops:
  4.6 169.6 %collective-permute-start = (bf16[16,15,4096]{2,0,1:T(8,128)(2,1)}, bf16[16,15,4096]{2,0,1:T(8,128)(2,1)}, u32[]{:S(2)}, u32[]{:S(2)}) collective-permute-start(bf16[16,15,4096]{2,0,1:T(8,128)(2,1)} %copy.107), channel_id=1, source_target_pairs={{0,1},{1,2},{2,3},{3,4},{4,5},{5,6},{6,7},{8,9},{9,10},{10,11},{11... | collective-permute-start | bytes 5898248 | tf_op jit(solution)/shard_map/ppermute | solution.py:15
  169.3 2.3 copy-start.7
  171.6 2.4 copy-start.10
  174.0 4.4 copy-start
  209.8 2.9 copy-start.9
  275.6 2.2 copy-start.1
  275.6 3.9 copy-start.2
  277.8 3.4 copy-start.3
  279.5 3.5 copy-start.4
  281.2 3.5 copy-start.5
  283.0 3.4 copy-start.6
  450.4 42.0 %all-to-all-start.1 = ((bf16[8,1,1,2,16,256,24]{5,6,4,3,2,1,0:T(8,128)(2,1)}), bf16[8,1,1,2,16,256,24]{5,6,4,3,2,1,0:T(8,128)(2,1)S(1)}, u32[]{:S(2)}, u32[]{:S(2)}) async-start(bf16[8,1,1,2,16,256,24]{5,6,4,3,2,1,0:T(8,128)(2,1)} %fusion.78), calls=%async_computation.1 | async-start | bytes 6291456 | tf_op jit(solution)/shard_map/all_to_all | solution.py:82
  454.8 2.7 copy-start.11
  454.8 2.7 copy-start.12
  562.5 22.7 %copy-start.8 = (s32[120]{0:T(128)S(1)}, s32[120]{0:T(128)}, u32[]{:S(2)}) copy-start(s32[120]{0:T(128)} %constant.106) | copy-start | bytes 1444
